TPU v7x, 32 devices: a whole 2x2x4 slice. The times are simulated.
32 devices in a mesh: ax: 8 (over z, y), az: 2 (over x), rad: 2 (over core).
Axes of the slice: x: 2, y: 2, z: 4, core: 2. Of those that a mesh axis runs over, the one named last changes fastest.
Arguments:
- state: float32 [5, 64, 128, 1024], P(None, 'ax', 'rad', 'az'), may hold values from -6 to 6
- section: float32 [5, 64, 128, 1024], P(None, 'ax', 'rad', 'az'), may hold values from -6 to 6
- mean_axial: float32 [128], P('rad'), may hold values from 0.3 to 0.6
- mean_swirl: float32 [128], P('rad'), may hold values from 0.1 to 0.4
- mean_density: float32 [128], P('rad'), may hold values from 0.8 to 1.25
- sound_squared: float32 [128], P('rad'), may hold values from 0.8 to 1.25
Outputs:
- new_state: float32 [5, 64, 128, 1024], P(None, 'ax', 'rad', 'az')
- new_section: float32 [5, 64, 128, 1024], P(None, 'ax', 'rad', 'az')
All inputs are finite; a program needn't handle non-finite values.
Results may differ from a plain program's by a relative error of at most 0.00005.
Values sent between devices are 32-bit elements; how exact they have to be, the bound alone decides.
A program may use at most 128 MiB of HBM per device.

v0:
```python
import functools
import math

import jax
import jax.numpy as jnp
import numpy as np
from jax import lax
from jax.experimental import pallas as pl
from jax.experimental.pallas import tpu as pltpu
from jax.sharding import PartitionSpec as P

NT = 1024
MESH = pl.DeviceIdType.MESH

drp_coeffs = (0.770882380518, -0.166705904415, 0.02084314277)
section_keep = -0.4178904745
section_gain = 0.3792103129999
time_step = 0.25
HALO = 3
RIM = 8


def spectral_tables(owners, local):
    s = np.arange(local)[:, None]
    t = np.arange(local)[None, :]
    tables = []
    for d in range(owners):
        spacing = (t - s + d * local) % NT
        spacing = np.where(spacing > NT // 2, spacing - NT, spacing)
        angle = np.pi * spacing / NT
        safe = np.where(spacing == 0, 1.0, np.sin(angle))
        parity = 1.0 - 2.0 * (spacing % 2)
        tables.append(np.where(spacing == 0, 0.0, 0.5 * parity * np.cos(angle) / safe))
    full = np.stack(tables).astype(np.float32)
    high = full.astype(jnp.bfloat16)
    low = (full - high.astype(np.float32)).astype(jnp.bfloat16)
    return np.stack([high, low], axis=1)


def kernel(
    sizes, state, section, axial_speed, swirl, density_in, sound, table_in, out_state, out_section,
    st, pr, other, ns, nst, coef, table, means,
    load_sem, az_send, az_recv, ax_send, ax_recv, rad_send, rad_recv, out_sem,
):
    n_ax, n_az, n_rad, count, rows, local = sizes
    ax = lax.axis_index("ax")
    az = lax.axis_index("az")
    rad = lax.axis_index("rad")
    has_prev, has_next = ax > 0, ax < n_ax - 1
    has_low, has_high = rad > 0, rad < n_rad - 1

    def az_copy(d, c):
        return pltpu.make_async_remote_copy(
            src_ref=state.at[:, c],
            dst_ref=other.at[d - 1, :, c],
            send_sem=az_send.at[d - 1, c],
            recv_sem=az_recv.at[d - 1, c],
            device_id={"az": lax.rem(az + d, n_az)},
            device_id_type=MESH,
        )

    def ax_copy(up):
        return pltpu.make_async_remote_copy(
            src_ref=state.at[:, pl.ds(count - HALO if up else 0, HALO)],
            dst_ref=st.at[:, pl.ds(0 if up else count + HALO, HALO)],
            send_sem=ax_send.at[0 if up else 1],
            recv_sem=ax_recv.at[0 if up else 1],
            device_id={"ax": ax + 1 if up else ax - 1},
            device_id_type=MESH,
        )

    def rad_copy(up, k):
        return pltpu.make_async_remote_copy(
            src_ref=state.at[2 + 2 * k, :, pl.ds(rows - RIM if up else 0, RIM)],
            dst_ref=pr.at[k, :, pl.ds(0 if up else rows + RIM, RIM)],
            send_sem=rad_send.at[0 if up else 1, k],
            recv_sem=rad_recv.at[0 if up else 1, k],
            device_id={"rad": rad + 1 if up else rad - 1},
            device_id_type=MESH,
        )

    loads = [
        pltpu.make_async_copy(state, st.at[:, pl.ds(HALO, count)], load_sem.at[0]),
        pltpu.make_async_copy(section, ns, load_sem.at[1]),
        pltpu.make_async_copy(state.at[2], pr.at[0, :, pl.ds(RIM, rows)], load_sem.at[2]),
        pltpu.make_async_copy(state.at[4], pr.at[1, :, pl.ds(RIM, rows)], load_sem.at[3]),
        pltpu.make_async_copy(table_in, table, load_sem.at[4]),
    ]
    vectors = [
        pltpu.make_async_copy(ref, means.at[i], load_sem.at[5 + i])
        for i, ref in enumerate((axial_speed, swirl, density_in, sound))
    ]
    for copy in vectors:
        copy.start()

    barrier = pltpu.get_barrier_semaphore()

    def greet(axis, index):
        pl.semaphore_signal(barrier, inc=1, device_id={axis: index}, device_id_type=MESH)

    for d in range(1, n_az):
        greet("az", lax.rem(az + d, n_az))
    pl.when(has_prev)(lambda: greet("ax", ax - 1))
    pl.when(has_next)(lambda: greet("ax", ax + 1))
    pl.when(has_low)(lambda: greet("rad", rad - 1))
    pl.when(has_high)(lambda: greet("rad", rad + 1))
    met = n_az - 1
    for there in (has_prev, has_next, has_low, has_high):
        met = met + there.astype(jnp.int32)
    pl.semaphore_wait(barrier, met)

    def send_plane(c, carry):
        for d in range(1, n_az):
            az_copy(d, c).start()
        return carry

    send_plane(0, 0)
    pl.when(has_next)(lambda: ax_copy(True).start())
    pl.when(has_prev)(lambda: ax_copy(False).start())
    for k in range(2):
        pl.when(has_high)(lambda: rad_copy(True, k).start())
        pl.when(has_low)(lambda: rad_copy(False, k).start())
    lax.fori_loop(1, count, send_plane, 0)
    for copy in loads:
        copy.start()

    for copy in vectors:
        copy.wait()

    pick = lax.broadcasted_iota(jnp.int32, (rows, rows), 0) == lax.broadcasted_iota(
        jnp.int32, (rows, rows), 1
    )

    def column(i):
        line = jnp.broadcast_to(means[i], (rows, rows))
        return jnp.sum(jnp.where(pick, line, 0.0), axis=1, keepdims=True)

    cell = lax.broadcasted_iota(jnp.int32, (rows, local), 0) + rad * rows
    inv_radius = 1.0 / (NT / (2.0 * math.pi) + cell.astype(jnp.float32) + 0.5)
    density = jnp.broadcast_to(column(2), (rows, local))
    minus = -time_step
    inverse = minus / density
    stiff = minus * density * column(3)
    coef[0] = jnp.broadcast_to(minus * column(0), (rows, local))
    coef[1] = minus * column(1) * inv_radius
    coef[2] = minus * density
    coef[3] = stiff
    coef[4] = inverse
    coef[5] = minus * density * inv_radius
    coef[6] = stiff * inv_radius
    coef[7] = inverse * inv_radius

    def azimuthal(values, d):
        flat = values.reshape(5 * rows, local)
        high = flat.astype(jnp.bfloat16)
        low = (flat - high.astype(jnp.float32)).astype(jnp.bfloat16)
        dot = functools.partial(jnp.dot, preferred_element_type=jnp.float32)
        g = dot(high, table[d, 0]) + dot(low, table[d, 0]) + dot(high, table[d, 1])
        return g.reshape(5, rows, local)

    def add_azimuthal(c, g):
        rate = coef[1]
        ns[0, c] += rate * g[0] + coef[5] * g[3]
        ns[1, c] += rate * g[1]
        ns[2, c] += rate * g[2]
        ns[3, c] += rate * g[3] + coef[7] * g[4]
        ns[4, c] += rate * g[4] + coef[6] * g[3]

    def radial(k, c):
        total = jnp.zeros((rows, local), jnp.float32)
        for j in range(1, 4):
            total += drp_coeffs[j - 1] * (
                pr[k, c, pl.ds(RIM + j, rows)] - pr[k, c, pl.ds(RIM - j, rows)]
            )
        return total

    def axial(f, c):
        total = jnp.zeros((rows, local), jnp.float32)
        for j in range(1, 4):
            total += drp_coeffs[j - 1] * (st[f, c + HALO + j] - st[f, c + HALO - j])
        return total

    for copy in loads:
        copy.wait()

    def wall(low):
        def fill(c, carry):
            for k, sign in enumerate((-1.0, 1.0)):
                for j in range(3):
                    if low:
                        pr[k, c, pl.ds(RIM - 1 - j, 1)] = sign * pr[k, c, pl.ds(RIM + j, 1)]
                    else:
                        pr[k, c, pl.ds(RIM + rows + j, 1)] = sign * pr[
                            k, c, pl.ds(RIM + rows - 1 - j, 1)
                        ]
            return carry

        lax.fori_loop(0, count, fill, 0)

    pl.when(jnp.logical_not(has_low))(lambda: wall(True))
    pl.when(jnp.logical_not(has_high))(lambda: wall(False))
    for k in range(2):
        pl.when(has_low)(lambda: rad_copy(True, k).wait_recv())
        pl.when(has_high)(lambda: rad_copy(False, k).wait_recv())

    def own_part(c, carry):
        for f in range(5):
            ns[f, c] = section_keep * ns[f, c]
        spread = radial(0, c)
        ns[0, c] += coef[2] * spread
        ns[4, c] += coef[3] * spread
        ns[2, c] += coef[4] * radial(1, c)
        add_azimuthal(c, azimuthal(st[:, HALO + c], 0))
        return carry

    lax.fori_loop(0, count, own_part, 0)

    def far_part(c, carry):
        def step(d, inner):
            az_copy(d, c).wait_recv()
            add_azimuthal(c, azimuthal(other[d - 1, :, c], d))
            return inner

        return lax.fori_loop(1, n_az, step, carry)

    def axial_part(c, carry):
        along = axial(1, c)
        press = axial(4, c)
        speed = coef[0]
        ns[0, c] += speed * axial(0, c) + coef[2] * along
        ns[1, c] += speed * along + coef[4] * press
        ns[2, c] += speed * axial(2, c)
        ns[3, c] += speed * axial(3, c)
        ns[4, c] += speed * press + coef[3] * along
        return carry

    def out_copies(c):
        return (
            pltpu.make_async_copy(ns.at[:, c], out_section.at[:, c], out_sem.at[0, c]),
            pltpu.make_async_copy(nst.at[:, c], out_state.at[:, c], out_sem.at[1, c]),
        )

    def finish(c, carry):
        for f in range(5):
            nst[f, c] = st[f, HALO + c] + section_gain * ns[f, c]
        for copy in out_copies(c):
            copy.start()
        return carry

    early = count - 2
    lax.fori_loop(0, early, far_part, 0)

    def clear(start):
        st[:, pl.ds(start, HALO)] = jnp.zeros((5, HALO, rows, local), jnp.float32)

    pl.when(has_prev)(lambda: ax_copy(True).wait_recv())
    pl.when(has_next)(lambda: ax_copy(False).wait_recv())
    pl.when(jnp.logical_not(has_prev))(lambda: clear(0))
    pl.when(jnp.logical_not(has_next))(lambda: clear(count + HALO))
    lax.fori_loop(0, count, axial_part, 0)
    lax.fori_loop(0, early, finish, 0)
    lax.fori_loop(early, count, lambda c, carry: finish(c, far_part(c, carry)), 0)

    def drain(c, carry):
        for copy in out_copies(c):
            copy.wait()
        for d in range(1, n_az):
            az_copy(d, c).wait_send()
        return carry

    lax.fori_loop(0, count, drain, 0)
    pl.when(has_next)(lambda: ax_copy(True).wait_send())
    pl.when(has_prev)(lambda: ax_copy(False).wait_send())
    for k in range(2):
        pl.when(has_high)(lambda: rad_copy(True, k).wait_send())
        pl.when(has_low)(lambda: rad_copy(False, k).wait_send())


def body(mesh_sizes, state, section, mean_axial, mean_swirl, mean_density, sound_squared):
    n_ax, n_az, n_rad = mesh_sizes
    _, count, rows, local = state.shape
    table = jnp.asarray(spectral_tables(n_az, local))
    whole = (5, count, rows, local)
    far = pl.BlockSpec(memory_space=pltpu.HBM)
    f32 = jnp.float32
    dma = pltpu.SemaphoreType.DMA
    return pl.pallas_call(
        functools.partial(kernel, (n_ax, n_az, n_rad, count, rows, local)),
        out_shape=(jax.ShapeDtypeStruct(whole, f32), jax.ShapeDtypeStruct(whole, f32)),
        in_specs=[far] * 7,
        out_specs=(far, far),
        scratch_shapes=[
            pltpu.VMEM((5, count + 2 * HALO, rows, local), f32),
            pltpu.VMEM((2, count, rows + 2 * RIM, local), f32),
            pltpu.VMEM((n_az - 1, 5, count, rows, local), f32),
            pltpu.VMEM(whole, f32),
            pltpu.VMEM(whole, f32),
            pltpu.VMEM((8, rows, local), f32),
            pltpu.VMEM((n_az, 2, local, local), jnp.bfloat16),
            pltpu.VMEM((4, 1, rows), f32),
            dma((9,)),
            dma((n_az - 1, count)),
            dma((n_az - 1, count)),
            dma((2,)),
            dma((2,)),
            dma((2, 2)),
            dma((2, 2)),
            dma((2, count)),
        ],
        compiler_params=pltpu.CompilerParams(
            collective_id=0, has_side_effects=True, vmem_limit_bytes=48 * 2**20
        ),
        cost_estimate=pl.CostEstimate(
            flops=6 * 5 * count * rows * local * NT,
            bytes_accessed=4 * 4 * 5 * count * rows * local,
            transcendentals=0,
        ),
    )(
        state,
        section,
        mean_axial[None],
        mean_swirl[None],
        mean_density[None],
        sound_squared[None],
        table,
    )


def solution(mesh):
    spec = P(None, "ax", "rad", "az")
    sizes = (mesh.shape["ax"], mesh.shape["az"], mesh.shape["rad"])
    return jax.shard_map(
        functools.partial(body, sizes),
        mesh=mesh,
        in_specs=(spec, spec, P("rad"), P("rad"), P("rad"), P("rad")),
        out_specs=(spec, spec),
        check_vma=False,
    )
```

profile of v0, /device:TPU:0, one launch (start us, length us, event | category | flops | bytes accessed | tf_op | source)
XLA Modules:
  0.0 132.9 jit_solution(14753999422424188388)
XLA Ops:
  0.6 0.0 copy-start
  0.6 0.6 copy-done
  1.3 0.0 copy-start.1
  1.3 0.7 copy-done.1
  1.9 0.0 copy-start.2
  1.9 0.7 copy-done.2
  2.6 0.0 copy-start.3
  2.6 0.7 copy-done.3
  3.3 0.0 copy-start.4
  3.3 1.6 %copy-done.4 = bf16[2,2,512,512]{3,2,1,0:T(8,128)(2,1)S(1)} copy-done((bf16[2,2,512,512]{3,2,1,0:T(8,128)(2,1)S(1)}, bf16[2,2,512,512]{3,2,1,0:T(8,128)(2,1)}, u32[]{:S(2)}) %copy-start.4) | copy-done | bytes 2097176
  4.8 119.7 %shard_map.86 = (f32[5,8,64,512]{3,2,1,0:T(8,128)}, f32[5,8,64,512]{3,2,1,0:T(8,128)}) custom-call(f32[5,8,64,512]{3,2,1,0:T(8,128)} %state.1, f32[5,8,64,512]{3,2,1,0:T(8,128)} %section.1, f32[1,64]{1,0:T(1,128)S(1)} %bitcast.4, f32[1,64]{1,0:T(1,128)S(1)} %bitcast.5, f32[1,64]{1,0:T(1,128)S(1)} %bitcast.6, f32[1,64]{1,0:T(1,128)S(1)} %bitcast.7, ...), custom_call_target="tpu_custom_call" | custom-call | flops 8053063680 | bytes 20971520 | tf_op jit(solution)/shard_map/pallas_call | solution.py:287
  124.6 0.0 copy-start.5
  124.6 6.0 %copy.11 = f32[5,8,64,512]{3,2,1,0:T(8,128)} copy(f32[5,8,64,512]{3,2,1,0:T(8,128)} %get-tuple-element.4) | data formatting | bytes 10485760
  130.6 0.0 copy-done.5
  130.6 2.4 %copy.12 = f32[5,8,64,512]{3,2,1,0:T(8,128)} copy(f32[5,8,64,512]{3,2,1,0:T(8,128)S(1)} %copy-done.5) | data formatting | bytes 10485760
Async XLA Ops:
  0.6 0.7 copy-start
  1.3 0.7 copy-start.1
  1.9 0.7 copy-start.2
  2.6 0.7 copy-start.3
  3.3 1.6 %copy-start.4 = (bf16[2,2,512,512]{3,2,1,0:T(8,128)(2,1)S(1)}, bf16[2,2,512,512]{3,2,1,0:T(8,128)(2,1)}, u32[]{:S(2)}) copy-start(bf16[2,2,512,512]{3,2,1,0:T(8,128)(2,1)} %constant.2.clone.table_in) | copy-start | bytes 6291460
  124.6 6.0 %copy-start.5 = (f32[5,8,64,512]{3,2,1,0:T(8,128)S(1)}, f32[5,8,64,512]{3,2,1,0:T(8,128)}, u32[]{:S(2)}) copy-start(f32[5,8,64,512]{3,2,1,0:T(8,128)} %get-tuple-element.5) | copy-start | bytes 15728644
where the time goes:
time: 133 us
  Pallas kernels  120 us (90%)
  local copies, waits for them, and re-layouts  12.6 us (9%)
    pallas_call x1, Pallas kernels, body(): pl.pallas_call(functools.partial(kernel, (n_ax, n_az, n_rad, count, rows,...  120 us
    unnamed x14, local copies, waits for them, and re-layouts  12.6 us

commit v1 on v0

--- a/solution.py
+++ b/solution.py
@@ -37,10 +37,29 @@
     return np.stack([high, low], axis=1)
 
 
+def azimuthal(values, high_table, low_table):
+    fields, rows, local = values.shape
+    flat = values.reshape(fields * rows, local)
+    high = flat.astype(jnp.bfloat16)
+    low = (flat - high.astype(jnp.float32)).astype(jnp.bfloat16)
+    dot = functools.partial(jnp.dot, preferred_element_type=jnp.float32)
+    g = dot(high, high_table) + dot(low, high_table) + dot(high, low_table)
+    return g.reshape(fields, rows, local)
+
+
+def add_azimuthal(ns, coef, c, g):
+    rate = coef[1]
+    ns[0, c] += rate * g[0] + coef[5] * g[3]
+    ns[1, c] += rate * g[1]
+    ns[2, c] += rate * g[2]
+    ns[3, c] += rate * g[3] + coef[7] * g[4]
+    ns[4, c] += rate * g[4] + coef[6] * g[3]
+
+
 def kernel(
-    sizes, state, section, axial_speed, swirl, density_in, sound, table_in, out_state, out_section,
-    st, pr, other, ns, nst, coef, table, means,
-    load_sem, az_send, az_recv, ax_send, ax_recv, rad_send, rad_recv, out_sem,
+    sizes, state, section, axial_speed, swirl, density_in, sound, table_in, ns, nst, late, coef,
+    st, pr, other, table, means,
+    load_sem, az_send, az_recv, ax_send, ax_recv, rad_send, rad_recv,
 ):
     n_ax, n_az, n_rad, count, rows, local = sizes
     ax = lax.axis_index("ax")
@@ -49,10 +68,10 @@
     has_prev, has_next = ax > 0, ax < n_ax - 1
     has_low, has_high = rad > 0, rad < n_rad - 1
 
-    def az_copy(d, c):
+    def az_copy(d, c, last=False):
         return pltpu.make_async_remote_copy(
             src_ref=state.at[:, c],
-            dst_ref=other.at[d - 1, :, c],
+            dst_ref=late.at[d - 1] if last else other.at[d - 1, :, c],
             send_sem=az_send.at[d - 1, c],
             recv_sem=az_recv.at[d - 1, c],
             device_id={"az": lax.rem(az + d, n_az)},
@@ -120,7 +139,9 @@
     for k in range(2):
         pl.when(has_high)(lambda: rad_copy(True, k).start())
         pl.when(has_low)(lambda: rad_copy(False, k).start())
-    lax.fori_loop(1, count, send_plane, 0)
+    lax.fori_loop(1, count - 1, send_plane, 0)
+    for d in range(1, n_az):
+        az_copy(d, count - 1, True).start()
     for copy in loads:
         copy.start()
 
@@ -150,22 +171,6 @@
     coef[6] = stiff * inv_radius
     coef[7] = inverse * inv_radius
 
-    def azimuthal(values, d):
-        flat = values.reshape(5 * rows, local)
-        high = flat.astype(jnp.bfloat16)
-        low = (flat - high.astype(jnp.float32)).astype(jnp.bfloat16)
-        dot = functools.partial(jnp.dot, preferred_element_type=jnp.float32)
-        g = dot(high, table[d, 0]) + dot(low, table[d, 0]) + dot(high, table[d, 1])
-        return g.reshape(5, rows, local)
-
-    def add_azimuthal(c, g):
-        rate = coef[1]
-        ns[0, c] += rate * g[0] + coef[5] * g[3]
-        ns[1, c] += rate * g[1]
-        ns[2, c] += rate * g[2]
-        ns[3, c] += rate * g[3] + coef[7] * g[4]
-        ns[4, c] += rate * g[4] + coef[6] * g[3]
-
     def radial(k, c):
         total = jnp.zeros((rows, local), jnp.float32)
         for j in range(1, 4):
@@ -210,7 +215,7 @@
         ns[0, c] += coef[2] * spread
         ns[4, c] += coef[3] * spread
         ns[2, c] += coef[4] * radial(1, c)
-        add_azimuthal(c, azimuthal(st[:, HALO + c], 0))
+        add_azimuthal(ns, coef, c, azimuthal(st[:, HALO + c], table[0, 0], table[0, 1]))
         return carry
 
     lax.fori_loop(0, count, own_part, 0)
@@ -218,7 +223,7 @@
     def far_part(c, carry):
         def step(d, inner):
             az_copy(d, c).wait_recv()
-            add_azimuthal(c, azimuthal(other[d - 1, :, c], d))
+            add_azimuthal(ns, coef, c, azimuthal(other[d - 1, :, c], table[d, 0], table[d, 1]))
             return inner
 
         return lax.fori_loop(1, n_az, step, carry)
@@ -234,17 +239,9 @@
         ns[4, c] += speed * press + coef[3] * along
         return carry
 
-    def out_copies(c):
-        return (
-            pltpu.make_async_copy(ns.at[:, c], out_section.at[:, c], out_sem.at[0, c]),
-            pltpu.make_async_copy(nst.at[:, c], out_state.at[:, c], out_sem.at[1, c]),
-        )
-
     def finish(c, carry):
         for f in range(5):
             nst[f, c] = st[f, HALO + c] + section_gain * ns[f, c]
-        for copy in out_copies(c):
-            copy.start()
         return carry
 
     early = count - 2
@@ -259,21 +256,65 @@
     pl.when(jnp.logical_not(has_next))(lambda: clear(count + HALO))
     lax.fori_loop(0, count, axial_part, 0)
     lax.fori_loop(0, early, finish, 0)
-    lax.fori_loop(early, count, lambda c, carry: finish(c, far_part(c, carry)), 0)
+    lax.fori_loop(early, count - 1, lambda c, carry: finish(c, far_part(c, carry)), 0)
+    for f in range(5):
+        nst[f, count - 1] = st[f, HALO + count - 1]
 
     def drain(c, carry):
-        for copy in out_copies(c):
-            copy.wait()
         for d in range(1, n_az):
             az_copy(d, c).wait_send()
         return carry
 
-    lax.fori_loop(0, count, drain, 0)
+    lax.fori_loop(0, count - 1, drain, 0)
     pl.when(has_next)(lambda: ax_copy(True).wait_send())
     pl.when(has_prev)(lambda: ax_copy(False).wait_send())
     for k in range(2):
         pl.when(has_high)(lambda: rad_copy(True, k).wait_send())
         pl.when(has_low)(lambda: rad_copy(False, k).wait_send())
+    for d in range(1, n_az):
+        az_copy(d, count - 1, True).wait_send()
+        az_copy(d, count - 1, True).wait_recv()
+
+
+def write_kernel(n_az, ns, nst, late, coef, table, out_state, out_section, fin, sem):
+    last = ns.shape[1] - 1
+
+    def copies(c):
+        return (
+            pltpu.make_async_copy(ns.at[:, c], out_section.at[:, c], sem.at[0, c]),
+            pltpu.make_async_copy(nst.at[:, c], out_state.at[:, c], sem.at[1, c]),
+        )
+
+    def begin(c, carry):
+        for copy in copies(c):
+            copy.start()
+        return carry
+
+    def end(c, carry):
+        for copy in copies(c):
+            copy.wait()
+        return carry
+
+    lax.fori_loop(0, last, begin, 0)
+
+    fin[:, 0] = ns[:, last]
+
+    def far_part(d, carry):
+        add_azimuthal(fin, coef, 0, azimuthal(late[d - 1], table[d, 0], table[d, 1]))
+        return carry
+
+    lax.fori_loop(1, n_az, far_part, 0)
+    for f in range(5):
+        fin[f, 1] = nst[f, last] + section_gain * fin[f, 0]
+    ends = (
+        pltpu.make_async_copy(fin.at[:, 0], out_section.at[:, last], sem.at[0, last]),
+        pltpu.make_async_copy(fin.at[:, 1], out_state.at[:, last], sem.at[1, last]),
+    )
+    for copy in ends:
+        copy.start()
+    lax.fori_loop(0, last, end, 0)
+    for copy in ends:
+        copy.wait()
 
 
 def body(mesh_sizes, state, section, mean_axial, mean_swirl, mean_density, sound_squared):
@@ -281,21 +322,22 @@
     _, count, rows, local = state.shape
     table = jnp.asarray(spectral_tables(n_az, local))
     whole = (5, count, rows, local)
+    late = (n_az - 1, 5, rows, local)
+    coef = (8, rows, local)
     far = pl.BlockSpec(memory_space=pltpu.HBM)
+    near = pl.BlockSpec(memory_space=pltpu.VMEM)
     f32 = jnp.float32
     dma = pltpu.SemaphoreType.DMA
-    return pl.pallas_call(
+    pin = functools.partial(pltpu.with_memory_space_constraint, memory_space=pltpu.HBM)
+    ns, nst, late, coef = pl.pallas_call(
         functools.partial(kernel, (n_ax, n_az, n_rad, count, rows, local)),
-        out_shape=(jax.ShapeDtypeStruct(whole, f32), jax.ShapeDtypeStruct(whole, f32)),
+        out_shape=tuple(pltpu.VMEM(shape, f32) for shape in (whole, whole, late, coef)),
         in_specs=[far] * 7,
-        out_specs=(far, far),
+        out_specs=(near,) * 4,
         scratch_shapes=[
             pltpu.VMEM((5, count + 2 * HALO, rows, local), f32),
             pltpu.VMEM((2, count, rows + 2 * RIM, local), f32),
-            pltpu.VMEM((n_az - 1, 5, count, rows, local), f32),
-            pltpu.VMEM(whole, f32),
-            pltpu.VMEM(whole, f32),
-            pltpu.VMEM((8, rows, local), f32),
+            pltpu.VMEM((n_az - 1, 5, count - 1, rows, local), f32),
             pltpu.VMEM((n_az, 2, local, local), jnp.bfloat16),
             pltpu.VMEM((4, 1, rows), f32),
             dma((9,)),
@@ -305,10 +347,9 @@
             dma((2,)),
             dma((2, 2)),
             dma((2, 2)),
-            dma((2, count)),
         ],
         compiler_params=pltpu.CompilerParams(
-            collective_id=0, has_side_effects=True, vmem_limit_bytes=48 * 2**20
+            collective_id=0, has_side_effects=True, vmem_limit_bytes=28 * 2**20
         ),
         cost_estimate=pl.CostEstimate(
             flops=6 * 5 * count * rows * local * NT,
@@ -316,14 +357,22 @@
             transcendentals=0,
         ),
     )(
-        state,
-        section,
-        mean_axial[None],
-        mean_swirl[None],
-        mean_density[None],
-        sound_squared[None],
-        table,
+        pin(state),
+        pin(section),
+        pin(mean_axial[None]),
+        pin(mean_swirl[None]),
+        pin(mean_density[None]),
+        pin(sound_squared[None]),
+        pin(table),
     )
+    return pl.pallas_call(
+        functools.partial(write_kernel, n_az),
+        out_shape=(jax.ShapeDtypeStruct(whole, f32), jax.ShapeDtypeStruct(whole, f32)),
+        in_specs=[near] * 5,
+        out_specs=(far, far),
+        scratch_shapes=[pltpu.VMEM((5, 2, rows, local), f32), dma((2, count))],
+        compiler_params=pltpu.CompilerParams(vmem_limit_bytes=8 * 2**20),
+    )(ns, nst, late, coef, table)
 
 
 def solution(mesh):

time: 133 us -> 123 us (0.925)
  local copies, waits for them, and re-layouts: 12.6 us -> 0.01 us
  Pallas kernels: 120 us -> 122 us
    unnamed x14 -> x2, local copies, waits for them, and re-layouts: 12.6 us -> 0.01 us
    pallas_call x0 -> x1, Pallas kernels: none -> 4.07 us  [body(): pl.pallas_call(functools.partial(write_kernel, n_az), out_shape=(jax.Shap...]
    pallas_call x1, Pallas kernels: 120 us -> 118 us  [body(): pl.pallas_call(functools.partial(kernel, (n_ax, n_az, n_rad, count, rows,...]
where the time goes in v1:
time: 123 us
  Pallas kernels  122 us (99%)
    pallas_call x1, Pallas kernels, body(): pl.pallas_call(functools.partial(kernel, (n_ax, n_az, n_rad, count, rows,...  118 us
    pallas_call x1, Pallas kernels, body(): pl.pallas_call(functools.partial(write_kernel, n_az), out_shape=(jax.Shap...  4.07 us

profile of v1, /device:TPU:0, one launch (start us, length us, event | category | flops | bytes accessed | tf_op | source)
XLA Modules:
  0.0 122.5 jit_solution(17233351707220776630)
XLA Ops:
  0.6 0.0 copy-start
  0.6 117.8 %shard_map.86 = (f32[5,8,64,512]{3,2,1,0:T(8,128)S(1)}, f32[5,8,64,512]{3,2,1,0:T(8,128)S(1)}, f32[1,5,64,512]{3,2,1,0:T(8,128)S(1)}, f32[8,64,512]{2,1,0:T(8,128)S(1)}) custom-call(f32[5,8,64,512]{3,2,1,0:T(8,128)} %state.1, f32[5,8,64,512]{3,2,1,0:T(8,128)} %section.1, f32[1,64]{1,0:T(1,128)} %bitcast.4, f32[1,64]{1,0:T(1,128)} %bitcast.5, ...), custom_call_target="tpu_custom_call" | custom-call | flops 8053063680 | bytes 20971520 | tf_op jit(solution)/shard_map/pallas_call | solution.py:332
  118.4 0.0 copy-done
  118.4 4.1 %shard_map.87 = (f32[5,8,64,512]{3,2,1,0:T(8,128)}, f32[5,8,64,512]{3,2,1,0:T(8,128)}) custom-call(f32[5,8,64,512]{3,2,1,0:T(8,128)S(1)} %get-tuple-element.6.ns, f32[5,8,64,512]{3,2,1,0:T(8,128)S(1)} %get-tuple-element.7.nst, f32[1,5,64,512]{3,2,1,0:T(8,128)S(1)} %get-tuple-element.8.late, f32[8,64,512]{2,1,0:T(8,128)S(1)} %get-tuple-element.9.coef, ...), custom_call_target="tpu_custom_call" | custom-call | tf_op jit(solution)/shard_map/pallas_call | solution.py:368
Async XLA Ops:
  0.6 117.8 %copy-start = (bf16[2,2,512,512]{3,2,1,0:T(8,128)(2,1)S(1)}, bf16[2,2,512,512]{3,2,1,0:T(8,128)(2,1)}, u32[]{:S(2)}) copy-start(bf16[2,2,512,512]{3,2,1,0:T(8,128)(2,1)} %constant.2.clone.table_in.table) | copy-start | bytes 6291460

commit v2 on v1

--- a/solution.py
+++ b/solution.py
@@ -109,20 +109,20 @@
         pltpu.make_async_copy(ref, means.at[i], load_sem.at[5 + i])
         for i, ref in enumerate((axial_speed, swirl, density_in, sound))
     ]
+
+    barrier = pltpu.get_barrier_semaphore()
+
+    def greet(axis, index):
+        pl.semaphore_signal(barrier, inc=1, device_id={axis: index}, device_id_type=MESH)
+
+    pl.when(has_prev)(lambda: greet("ax", ax - 1))
+    pl.when(has_next)(lambda: greet("ax", ax + 1))
+    for d in range(1, n_az):
+        greet("az", lax.rem(az + d, n_az))
+    pl.when(has_low)(lambda: greet("rad", rad - 1))
+    pl.when(has_high)(lambda: greet("rad", rad + 1))
     for copy in vectors:
         copy.start()
-
-    barrier = pltpu.get_barrier_semaphore()
-
-    def greet(axis, index):
-        pl.semaphore_signal(barrier, inc=1, device_id={axis: index}, device_id_type=MESH)
-
-    for d in range(1, n_az):
-        greet("az", lax.rem(az + d, n_az))
-    pl.when(has_prev)(lambda: greet("ax", ax - 1))
-    pl.when(has_next)(lambda: greet("ax", ax + 1))
-    pl.when(has_low)(lambda: greet("rad", rad - 1))
-    pl.when(has_high)(lambda: greet("rad", rad + 1))
     met = n_az - 1
     for there in (has_prev, has_next, has_low, has_high):
         met = met + there.astype(jnp.int32)

time: 123 us -> 123 us (level)
  no operation moved by 1% of the time
where the time goes in v2:
time: 123 us
  Pallas kernels  122 us (99%)
    pallas_call x1, Pallas kernels, body(): pl.pallas_call(functools.partial(kernel, (n_ax, n_az, n_rad, count, rows,...  118 us
    pallas_call x1, Pallas kernels, body(): pl.pallas_call(functools.partial(write_kernel, n_az), out_shape=(jax.Shap...  4.07 us

profile of v2, /device:TPU:0, one launch (start us, length us, event | category | flops | bytes accessed | tf_op | source)
XLA Modules:
  0.0 122.5 jit_solution(2904303137650100781)
XLA Ops:
  0.6 0.0 copy-start
  0.6 117.8 %shard_map.86 = (f32[5,8,64,512]{3,2,1,0:T(8,128)S(1)}, f32[5,8,64,512]{3,2,1,0:T(8,128)S(1)}, f32[1,5,64,512]{3,2,1,0:T(8,128)S(1)}, f32[8,64,512]{2,1,0:T(8,128)S(1)}) custom-call(f32[5,8,64,512]{3,2,1,0:T(8,128)} %state.1, f32[5,8,64,512]{3,2,1,0:T(8,128)} %section.1, f32[1,64]{1,0:T(1,128)} %bitcast.4, f32[1,64]{1,0:T(1,128)} %bitcast.5, ...), custom_call_target="tpu_custom_call" | custom-call | flops 8053063680 | bytes 20971520 | tf_op jit(solution)/shard_map/pallas_call | solution.py:332
  118.4 0.0 copy-done
  118.4 4.1 %shard_map.87 = (f32[5,8,64,512]{3,2,1,0:T(8,128)}, f32[5,8,64,512]{3,2,1,0:T(8,128)}) custom-call(f32[5,8,64,512]{3,2,1,0:T(8,128)S(1)} %get-tuple-element.6.ns, f32[5,8,64,512]{3,2,1,0:T(8,128)S(1)} %get-tuple-element.7.nst, f32[1,5,64,512]{3,2,1,0:T(8,128)S(1)} %get-tuple-element.8.late, f32[8,64,512]{2,1,0:T(8,128)S(1)} %get-tuple-element.9.coef, ...), custom_call_target="tpu_custom_call" | custom-call | tf_op jit(solution)/shard_map/pallas_call | solution.py:368
Async XLA Ops:
  0.6 117.8 %copy-start = (bf16[2,2,512,512]{3,2,1,0:T(8,128)(2,1)S(1)}, bf16[2,2,512,512]{3,2,1,0:T(8,128)(2,1)}, u32[]{:S(2)}) copy-start(bf16[2,2,512,512]{3,2,1,0:T(8,128)(2,1)} %constant.2.clone.table_in.table) | copy-start | bytes 6291460
